TPU v7x, 32 devices: a whole 2x2x4 slice. The times are simulated.
32 devices in a mesh: section: 4 (over y, x), ctx: 8 (over z, core).
Axes of the slice: x: 2, y: 2, z: 4, core: 2. Of those that a mesh axis runs over, the one named last changes fastest.
Arguments:
- projected: bfloat16 [4, 3072, 3072], P('section', 'ctx'), may hold values from -64 to 64
- grad_out: bfloat16 [4, 3072, 3072], P('section', 'ctx'), may hold values from -6 to 6
- doc_lengths: int32 [7], replicated, may hold values from 1 to 768, as said below
Outputs:
- grad_kv: float32 [3072, 2048], P('ctx')
Inputs may be any that keep to these rules, and one draw needn't show every extreme that they name: `doc_lengths`: the lengths sum to 3072; the first document is shorter than 384 tokens and the second has exactly 768.
All inputs are finite; a program needn't handle non-finite values.
Results may differ from a plain program's by a relative error of at most 0.0031.
Values may be sent and summed in bfloat16 or wider, within the bound.
A program may use at most 128 MiB of HBM per device.

v0:
```python
import math

import jax
import jax.numpy as jnp
from jax import lax
from jax.sharding import PartitionSpec as P

HEAD_SIZE = 128
KV_HEAD_COUNT = 8
QUERY_PER_KV = 3
REACH = 2


MASKED_SCORE = -1e30


def spread(value, axis, source):
    kept = jnp.where(lax.axis_index(axis) == source, value, 0).astype(value.dtype)
    return lax.psum(kept, axis)


def shifted(value, axis, steps):
    count = lax.axis_size(axis)
    leading, last = (max(0, -steps), min(count, count - steps))
    return lax.ppermute(value, axis, [(source, source + steps) for source in range(leading, last)])


def document_of(places, doc_ends):
    return jnp.sum((doc_ends[None, :] <= places[:, None]).astype(jnp.int32), axis=1)


def piece_scores(query_group, key_part, piece_mask, score_scale):
    scores = (
        jnp.einsum("qah,kh->aqk", query_group, key_part, preferred_element_type=jnp.float32)
        * score_scale
    )
    return jnp.where(piece_mask[None], scores, MASKED_SCORE)


def piece_attend(weight_part, value_part):
    return jnp.einsum("aqk,kh->qah", weight_part, value_part, preferred_element_type=jnp.float32)


def piece_grads(
    prob_part, weight_part, query_group, grad_group, value_part, delta_rows, score_scale
):
    grad_value = jnp.einsum(
        "aqk,qah->kh", weight_part, grad_group, preferred_element_type=jnp.float32
    )
    grad_prob = jnp.einsum(
        "qah,kh->aqk", grad_group, value_part, preferred_element_type=jnp.float32
    )
    grad_score = (prob_part * (grad_prob - delta_rows)).astype(jnp.bfloat16)
    grad_key = (
        jnp.einsum("aqk,qah->kh", grad_score, query_group, preferred_element_type=jnp.float32)
        * score_scale
    )
    return (grad_key, grad_value)


def on_device(projected, grad_out, doc_lengths):
    tok_rows = projected.shape[1]
    head_dim = HEAD_SIZE
    shared_key_heads = KV_HEAD_COUNT
    group = QUERY_PER_KV
    shared_width = shared_key_heads * head_dim
    out_width = 2 * shared_width
    reaching = REACH
    pieces = reaching + 1
    score_scale = 1.0 / math.sqrt(head_dim)
    shared = spread(projected[0][:, :out_width], "section", 0)
    earlier = []
    for distance in range(reaching, 0, -1):
        earlier.append(shifted(shared, "ctx", distance))
    window = jnp.concatenate(earlier + [shared], axis=0)
    key_heads = window[:, :shared_width].reshape(pieces * tok_rows, shared_key_heads, head_dim)
    value_heads = window[:, shared_width:].reshape(pieces * tok_rows, shared_key_heads, head_dim)
    queries = projected[0].reshape(tok_rows, shared_key_heads, group, head_dim)
    grad_heads = grad_out[0].reshape(tok_rows, shared_key_heads, group, head_dim)
    doc_ends = jnp.cumsum(doc_lengths)
    ctx_index = lax.axis_index("ctx")
    query_place = ctx_index * tok_rows + jnp.arange(tok_rows, dtype=jnp.int32)
    key_place = (ctx_index - reaching) * tok_rows + jnp.arange(pieces * tok_rows, dtype=jnp.int32)
    same_doc = (
        document_of(query_place, doc_ends)[:, None] == document_of(key_place, doc_ends)[None, :]
    )
    allowed = same_doc & (key_place[None, :] <= query_place[:, None]) & (key_place[None, :] >= 0)

    def group_grads(kv_index):
        query_group = lax.dynamic_index_in_dim(queries, kv_index, 1, keepdims=False)
        grad_group = lax.dynamic_index_in_dim(grad_heads, kv_index, 1, keepdims=False)
        key_group = lax.dynamic_index_in_dim(key_heads, kv_index, 1, keepdims=False)
        value_group = lax.dynamic_index_in_dim(value_heads, kv_index, 1, keepdims=False)
        score_parts = []
        for index in range(pieces):
            rows = slice(index * tok_rows, (index + 1) * tok_rows)
            score_parts.append(
                piece_scores(query_group, key_group[rows], allowed[:, rows], score_scale)
            )
        scores = jnp.concatenate(score_parts, axis=2)
        row_top = jnp.max(scores, axis=2, keepdims=True)
        powers = jnp.exp(scores - row_top)
        attn_weight = powers / jnp.sum(powers, axis=2, keepdims=True)
        attn_half = attn_weight.astype(jnp.bfloat16)
        attended = jnp.zeros((tok_rows, group, head_dim), jnp.float32)
        for index in range(pieces):
            rows = slice(index * tok_rows, (index + 1) * tok_rows)
            attended = attended + piece_attend(attn_half[:, :, rows], value_group[rows])
        delta_rows = jnp.sum(grad_group.astype(jnp.float32) * attended, axis=2).T[:, :, None]
        key_parts = []
        value_parts = []
        for index in range(pieces):
            rows = slice(index * tok_rows, (index + 1) * tok_rows)
            grad_key, grad_value = piece_grads(
                attn_weight[:, :, rows],
                attn_half[:, :, rows],
                query_group,
                grad_group,
                value_group[rows],
                delta_rows,
                score_scale,
            )
            key_parts.append(grad_key)
            value_parts.append(grad_value)
        return (jnp.concatenate(key_parts, axis=0), jnp.concatenate(value_parts, axis=0))

    key_grads, value_grads = lax.map(group_grads, jnp.arange(shared_key_heads, dtype=jnp.int32))
    is_cross = (lax.axis_index("section") > 0).astype(jnp.float32)
    key_flat = jnp.transpose(key_grads, (1, 0, 2)).reshape(pieces * tok_rows, shared_width)
    value_flat = jnp.transpose(value_grads, (1, 0, 2)).reshape(pieces * tok_rows, shared_width)
    grad_pieces = (jnp.concatenate([key_flat, value_flat], axis=1) * is_cross).reshape(
        pieces, tok_rows, out_width
    )
    summed = grad_pieces[reaching]
    for distance in range(1, reaching + 1):
        summed = summed + shifted(grad_pieces[reaching - distance], "ctx", -distance)
    return lax.psum(summed, "section")


def solution(mesh):
    return jax.shard_map(
        on_device,
        mesh=mesh,
        in_specs=(P("section", "ctx", None), P("section", "ctx", None), P()),
        out_specs=P("ctx", None),
        check_vma=False,
    )
```

profile of v0, /device:TPU:0, one launch (start us, length us, event | category | flops | bytes accessed | tf_op | source)
XLA Modules:
  0.0 582.2 jit_solution(11349256807391331822)
XLA Ops:
  6.5 4.3 copy.52
  10.8 2.9 slice_select_fusion
  13.8 63.7 %all-reduce.3.cloned.1.call-done = bf16[384,2048]{0,1:T(8,128)(2,1)} async-done(((bf16[384,2048]{0,1:T(8,128)(2,1)}), bf16[384,2048]{0,1:T(8,128)(2,1)}) %all-reduce.3.cloned.1.call-update) | async-done | bytes 1572880 | tf_op jit(solution)/shard_map/psum | solution.py:19
  77.4 4.5 collective-permute-start
  82.0 2.6 collective-permute-start.1
  84.8 2.4 copy.54
  87.4 2.0 and_and_fusion
  89.4 26.5 %collective-permute-done = bf16[384,2048]{0,1:T(8,128)(2,1)} collective-permute-done((bf16[384,2048]{0,1:T(8,128)(2,1)}, bf16[384,2048]{0,1:T(8,128)(2,1)}, u32[]{:S(2)}, u32[]{:S(2)}) %collective-permute-start) | collective-permute-done | bytes 1572896 | tf_op jit(solution)/shard_map/ppermute | solution.py:25
  115.9 1.6 constant_dynamic-update-slice_fusion.2
  117.5 1.7 constant_dynamic-update-slice_fusion.1
  119.6 2.5 fusion.71
  122.1 224.7 %while.12 = (s32[]{:T(128)}, f32[8,1152,128]{2,1,0:T(8,128)}, f32[8,1152,128]{2,1,0:T(8,128)}, pred[384,1152]{0,1:T(8,128)(4,1)}, s32[8]{0:T(128)S(1)}, /*index=...) while((s32[]{:T(128)}, f32[8,1152,128]{2,1,0:T(8,128)}, ...), condition=%wide.region_10.11_spmd, body=%wide.region_4.10_spmd.sunk | while | flops 1720070784 | bytes 68940056 | solution.py:127
  127.4 1.5 fusion.118
  131.2 3.7 fusion.121
  139.0 1.9 fusion.123
  140.9 2.3 fusion.126
  143.2 2.4 fusion.125
  145.6 2.3 fusion.124
  159.3 3.7 fusion.121
  167.0 1.9 fusion.123
  168.9 2.3 fusion.126
  171.2 2.4 fusion.125
  173.7 2.3 fusion.124
  187.3 3.7 fusion.121
  195.1 1.9 fusion.123
  197.0 2.3 fusion.126
  199.3 2.4 fusion.125
  201.7 2.3 fusion.124
  210.1 1.5 fusion.117
  215.5 3.7 fusion.121
  223.3 1.9 fusion.123
  225.1 2.3 fusion.126
  227.4 2.4 fusion.125
  229.9 2.3 fusion.124
  238.2 1.5 fusion.117
  239.7 1.5 fusion.118
  243.5 3.7 fusion.121
  251.3 1.9 fusion.123
  253.2 2.3 fusion.126
  255.5 2.4 fusion.125
  257.9 2.3 fusion.124
  267.8 1.5 fusion.118
  271.6 3.7 fusion.121
  279.4 1.9 fusion.123
  281.3 2.3 fusion.126
  283.6 2.4 fusion.125
  286.0 2.3 fusion.124
  299.7 3.7 fusion.121
  307.5 1.9 fusion.123
  309.4 2.3 fusion.126
  311.7 2.4 fusion.125
  314.1 2.3 fusion.124
  327.8 3.7 fusion.121
  335.6 1.9 fusion.123
  337.5 2.3 fusion.126
  339.8 2.4 fusion.125
  342.2 2.3 fusion.124
  346.8 8.7 %copy_bitcast_fusion = (f32[1152,1024]{1,0:T(8,128)}, f32[1152,1024]{1,0:T(8,128)}) fusion(f32[8,1152,128]{2,1,0:T(8,128)} %get-tuple-element.53, f32[8,1152,128]{2,1,0:T(8,128)} %get-tuple-element.54), kind=kLoop, calls=%fused_computation.83 | loop fusion | bytes 18874368 | tf_op jit(solution)/shard_map/reshape | solution.py:130
  355.5 4.9 maximum_multiply_fusion
  363.7 18.7 %collective-permute-done.2 = f32[384,2048]{1,0:T(8,128)S(1)} collective-permute-done((f32[384,2048]{1,0:T(8,128)S(1)}, f32[384,2048]{1,0:T(8,128)S(1)}, u32[]{:S(2)}, u32[]{:S(2)}) %collective-permute-start.2) | collective-permute-done | bytes 3145760 | tf_op jit(solution)/shard_map/ppermute | solution.py:25
  382.4 99.9 %collective-permute-done.3 = f32[384,2048]{1,0:T(8,128)S(1)} collective-permute-done((f32[384,2048]{1,0:T(8,128)S(1)}, f32[384,2048]{1,0:T(8,128)S(1)}, u32[]{:S(2)}, u32[]{:S(2)}) %collective-permute-start.3) | collective-permute-done | bytes 3145760 | tf_op jit(solution)/shard_map/ppermute | solution.py:25
  482.3 2.7 fusion.63
  485.0 86.4 %all-reduce.5.cloned.1.call-done = f32[384,2048]{1,0:T(8,128)} async-done(((f32[384,2048]{1,0:T(8,128)}), f32[384,2048]{1,0:T(8,128)}) %all-reduce.5.cloned.1.call-update) | async-done | bytes 3145744 | tf_op jit(solution)/shard_map/psum | solution.py:137
  571.4 3.9 copy.104
  (171 shorter events, 104.3 us)
Async XLA Ops:
  6.5 70.9 %all-reduce.3.cloned.1.call-start = ((), (), s32[]{:S(2)}) async-start(), calls=%async_computation | async-start | bytes 3145728 | tf_op jit(solution)/shard_map/psum | solution.py:19
  10.8 73.8 %copy-start.4 = (s32[7]{0:T(128)S(1)}, s32[7]{0:T(128)}, u32[]{:S(2)}) copy-start(s32[7]{0:T(128)} %param.7) | copy-start | bytes 88
  10.8 73.9 %copy-start.2 = (bf16[1,384,3072]{2,1,0:T(8,128)(2,1)S(1)}, bf16[1,384,3072]{2,1,0:T(8,128)(2,1)}, u32[]{:S(2)}) copy-start(bf16[1,384,3072]{2,1,0:T(8,128)(2,1)} %param.6) | copy-start | bytes 7077892
  13.7 557.7 %all-reduce.5.cloned.1.call-start = ((), (), s32[]{:S(2)}) async-start(), calls=%async_computation.1 | async-start | bytes 6291456 | tf_op jit(solution)/shard_map/psum | solution.py:137
  77.4 38.5 %collective-permute-start = (bf16[384,2048]{0,1:T(8,128)(2,1)}, bf16[384,2048]{0,1:T(8,128)(2,1)}, u32[]{:S(2)}, u32[]{:S(2)}) collective-permute-start(bf16[384,2048]{0,1:T(8,128)(2,1)} %all-reduce.3.cloned.1.call-done), channel_id=1, source_target_pairs={{0,2},{1,3},{2,4},{3,5},{4,6},{5,7},{8,10},{9,11},{10,12},{11,13},... | collective-permute-start | bytes 4718600 | tf_op jit(solution)/shard_map/ppermute | solution.py:25
  82.0 35.5 %collective-permute-start.1 = (bf16[384,2048]{0,1:T(8,128)(2,1)}, bf16[384,2048]{0,1:T(8,128)(2,1)}, u32[]{:S(2)}, u32[]{:S(2)}) collective-permute-start(bf16[384,2048]{0,1:T(8,128)(2,1)} %all-reduce.3.cloned.1.call-done), channel_id=1, source_target_pairs={{0,1},{1,2},{2,3},{3,4},{4,5},{5,6},{6,7},{8,9},{9,10},{10,11},{11... | collective-permute-start | bytes 4718600 | tf_op jit(solution)/shard_map/ppermute | solution.py:25
  89.4 29.8 %copy-start.3 = (bf16[384,2048]{0,1:T(8,128)(2,1)S(1)}, bf16[384,2048]{0,1:T(8,128)(2,1)}, u32[]{:S(2)}) copy-start(bf16[384,2048]{0,1:T(8,128)(2,1)} %all-reduce.3.cloned.1.call-done) | copy-start | bytes 4718596
  134.9 1.5 copy-start
  143.1 4.7 copy-start.1
  163.0 1.5 copy-start
  171.2 4.7 copy-start.1
  191.0 1.5 copy-start
  199.3 4.7 copy-start.1
  219.2 1.5 copy-start
  227.4 4.7 copy-start.1
  247.2 1.5 copy-start
  255.5 4.7 copy-start.1
  275.3 1.5 copy-start
  283.6 4.7 copy-start.1
  303.4 1.5 copy-start
  311.7 4.7 copy-start.1
  331.5 1.5 copy-start
  339.8 4.7 copy-start.1
  361.1 21.3 %collective-permute-start.2 = (f32[384,2048]{1,0:T(8,128)S(1)}, f32[384,2048]{1,0:T(8,128)S(1)}, u32[]{:S(2)}, u32[]{:S(2)}) collective-permute-start(f32[384,2048]{1,0:T(8,128)S(1)} %get-tuple-element.113), channel_id=1, source_target_pairs={{1,0},{2,1},{3,2},{4,3},{5,4},{6,5},{7,6},{9,8},{10,9},{11,10},{12... | collective-permute-start | bytes 9437192 | tf_op jit(solution)/shard_map/ppermute | solution.py:25
  362.4 119.9 %collective-permute-start.3 = (f32[384,2048]{1,0:T(8,128)S(1)}, f32[384,2048]{1,0:T(8,128)S(1)}, u32[]{:S(2)}, u32[]{:S(2)}) collective-permute-start(f32[384,2048]{1,0:T(8,128)S(1)} %get-tuple-element.114), channel_id=1, source_target_pairs={{2,0},{3,1},{4,2},{5,3},{6,4},{7,5},{10,8},{11,9},{12,10},{13,11},... | collective-permute-start | bytes 9437192 | tf_op jit(solution)/shard_map/ppermute | solution.py:25
Sparse Core Ops, SparseCore 0:
  13.8 63.5 all-reduce.2
  485.1 86.2 all-reduce.4
where the time goes:
time: 585 us; the launch traced here: 582 us
  waiting for transfers between devices  295 us (50%)
  matrix products  140 us (24%)
  other arithmetic  57.2 us (10%)
  local copies, waits for them, and re-layouts  50.4 us (9%)
  loops' own time  16.4 us (3%)
  between operations  13.5 us (2%)
  starting transfers between devices  9.75 us (2%)
    ppermute x4, waiting for transfers between devices, shifted(): lax.ppermute(value, axis, [(source, source + steps) for source in range(l...  145 us
    psum x1, waiting for transfers between devices, on_device(): return lax.psum(summed, 'section')  86.4 us
    psum x1, waiting for transfers between devices, spread(): return lax.psum(kept, axis)  63.7 us
    dot_general x24, matrix products, piece_grads(): jnp.einsum('aqk,qah->kh', grad_score, query_group, preferred_element_type...  55.7 us
    dot_general x24, matrix products, piece_attend(): jnp.einsum('aqk,kh->qah', weight_part, value_part, preferred_element_type...  37.8 us
    dot_general x24, matrix products, piece_scores(): jnp.einsum('qah,kh->aqk', query_group, key_part, preferred_element_type=j...  36.8 us
    convert_element_type x8, other arithmetic, group_grads(): attn_half = attn_weight.astype(jnp.bfloat16)  29.6 us
    another operation x1, loops' own time, on_device(): lax.map(group_grads, jnp.arange(shared_key_heads, dtype=jnp.int32))  16.4 us
  transfers between devices with their start and end apart: 6, of which 5 were waited for; matrix products, arithmetic and copies ran while one was open for 1% of the time, Pallas kernels for 0%

commit v1 on v0

v1 whole, which is shorter than its diff:
```python
import functools
import math

import jax
import jax.numpy as jnp
from jax import lax
from jax.experimental import pallas as pl
from jax.experimental.pallas import tpu as pltpu
from jax.sharding import PartitionSpec as P

HEAD_SIZE = 128
KV_HEAD_COUNT = 8
QUERY_PER_KV = 3
REACH = 2
ROWS = 128
AHEAD = 3
MASKED_SCORE = -1e30
MESH = pl.DeviceIdType.MESH


def ring_swap(place, sections):
    half = sections // 2
    back = place // half
    return place * (1 - back) + back * (half + sections - 1 - place)


def dot_last(left, right):
    return lax.dot_general(
        left, right, (((1,), (1,)), ((), ())), preferred_element_type=jnp.float32
    )


def folded(value, reduce):
    return reduce(value.reshape(-1, 8, value.shape[-1]), axis=0)


def kernel(
    sections,
    blocks,
    lengths_ref,
    projected_ref,
    grad_out_ref,
    out_ref,
    queries,
    cotangents,
    window,
    bias,
    score_buf,
    prob_grad_buf,
    grads,
    pair_in,
    hop_out,
    hop_in,
    part_out,
    part_in,
    final,
    load_sem,
    ring_send,
    ring_recv,
    hop_kv_send,
    hop_kv_recv,
    pair_kv_send,
    pair_kv_recv,
    pair_send,
    pair_recv,
    hop_send,
    hop_recv,
    part_send,
    part_recv,
    spread_send,
    spread_recv,
    store_sem,
):
    section = lax.axis_index("section")
    block = lax.axis_index("ctx")
    odd = lax.rem(block, 2)
    partner = block + 1 - 2 * odd
    place = ring_swap(section, sections)
    heads = KV_HEAD_COUNT
    tokens = out_ref.shape[0]
    width = heads * HEAD_SIZE
    group_width = QUERY_PER_KV * HEAD_SIZE
    span = REACH * tokens + ROWS
    scale = 1.0 / math.sqrt(HEAD_SIZE)
    exponent_scale = scale * math.log2(math.e)
    cross = section > 0
    has_before = block >= REACH
    has_after = block + REACH < blocks

    def block_rows(index):
        return pl.ds(index * tokens, tokens)

    def load_shared(head, kind):
        return pltpu.make_async_copy(
            projected_ref.at[:, pl.ds(kind * width + head * HEAD_SIZE, HEAD_SIZE)],
            window.at[head, kind, block_rows(REACH), :],
            load_sem.at[head, kind],
        )

    def load_group(head, kind):
        source, target = ((projected_ref, queries), (grad_out_ref, cotangents))[kind]
        return pltpu.make_async_copy(
            source.at[:, pl.ds(head * group_width, group_width)],
            target.at[head],
            load_sem.at[head, kind],
        )

    def ring_copy(head, kind):
        target_place = lax.rem(place + 1 - 2 * kind + sections, sections)
        own = window.at[head, kind, block_rows(REACH), :]
        return pltpu.make_async_remote_copy(
            src_ref=own,
            dst_ref=own,
            send_sem=ring_send.at[head, kind],
            recv_sem=ring_recv.at[head, kind],
            device_id={"section": ring_swap(target_place, sections), "ctx": block},
            device_id_type=MESH,
        )

    def ring_goes_on(kind):
        return lax.rem(place + 1 - 2 * kind + sections, sections) != 0

    def to_block(source, target, send_sem, recv_sem, target_block):
        return pltpu.make_async_remote_copy(
            src_ref=source,
            dst_ref=target,
            send_sem=send_sem,
            recv_sem=recv_sem,
            device_id={"section": section, "ctx": target_block},
            device_id_type=MESH,
        )

    def hop_kv(head):
        return to_block(
            window.at[head, :, block_rows(REACH), :],
            window.at[head, :, block_rows(0), :],
            hop_kv_send.at[head],
            hop_kv_recv.at[head],
            block + REACH,
        )

    def pair_kv(head, source_block):
        return to_block(
            window.at[head, :, block_rows(source_block), :],
            window.at[head, :, block_rows(1), :],
            pair_kv_send.at[head],
            pair_kv_recv.at[head],
            partner,
        )

    def pair_grads(head):
        return to_block(
            grads.at[head, :, block_rows(1), :],
            pair_in.at[head],
            pair_send.at[head],
            pair_recv.at[head],
            partner,
        )

    def hop_grads(head):
        return to_block(
            hop_out.at[head], hop_in.at[head], hop_send.at[head], hop_recv.at[head], block - REACH
        )

    def part_copy(head, source, target):
        return pltpu.make_async_remote_copy(
            src_ref=part_out.at[head],
            dst_ref=part_in.at[head // sections, source],
            send_sem=part_send.at[head],
            recv_sem=part_recv.at[head // sections, source],
            device_id={"section": target, "ctx": block},
            device_id_type=MESH,
        )

    def out_columns(head, kind):
        start = pl.multiple_of(kind * width + head * HEAD_SIZE, HEAD_SIZE)
        return out_ref.at[:, pl.ds(start, HEAD_SIZE)]

    def spread_copy(head, kind, target):
        return pltpu.make_async_remote_copy(
            src_ref=final.at[head // sections, kind],
            dst_ref=out_columns(head, kind),
            send_sem=spread_send.at[head // sections, target, kind],
            recv_sem=spread_recv.at[head, kind],
            device_id={"section": target, "ctx": block},
            device_id_type=MESH,
        )

    def store_copy(head, kind):
        return pltpu.make_async_copy(
            final.at[head // sections, kind],
            out_columns(head, kind),
            store_sem.at[head // sections, kind],
        )

    @pl.when(section == 0)
    def _():
        for head in range(heads):
            for kind in range(2):
                load_shared(head, kind).start()

    @pl.when(cross)
    def _():
        for head in range(heads):
            for kind in range(2):
                load_group(head, kind).start()

    barrier = pltpu.get_barrier_semaphore()
    for step in range(1, sections):
        pl.semaphore_signal(
            barrier,
            inc=1,
            device_id={"section": lax.rem(section + step, sections), "ctx": block},
            device_id_type=MESH,
        )
    pl.semaphore_signal(
        barrier, inc=1, device_id={"section": section, "ctx": partner}, device_id_type=MESH
    )

    @pl.when(has_before)
    def _():
        pl.semaphore_signal(
            barrier,
            inc=1,
            device_id={"section": section, "ctx": block - REACH},
            device_id_type=MESH,
        )

    @pl.when(has_after)
    def _():
        pl.semaphore_signal(
            barrier,
            inc=1,
            device_id={"section": section, "ctx": block + REACH},
            device_id_type=MESH,
        )

    before_count = jnp.where(has_before, 1, 0)
    after_count = jnp.where(has_after, 1, 0)
    pl.semaphore_wait(barrier, sections + before_count + after_count)

    def finish(head):
        slot = head // sections
        for kind in range(2):

            @pl.when(cross)
            def _():
                final[slot, kind] = grads[head, kind, block_rows(REACH), :]

            @pl.when(section == 0)
            def _():
                final[slot, kind] = jnp.zeros((tokens, HEAD_SIZE), jnp.float32)

        for source in range(1, sections):

            @pl.when(section != source)
            def _():
                part_copy(head, source, section).wait_recv()
                final[slot] += part_in[slot, source].astype(jnp.float32)

        final[slot, 0] *= scale
        for kind in range(2):
            store_copy(head, kind).start()
            for step in range(1, sections):
                spread_copy(head, kind, lax.rem(section + step, sections)).start()

    @pl.when(section == 0)
    def _():
        for head in range(heads):
            for kind in range(2):
                load_shared(head, kind).wait()
                ring_copy(head, kind).start()

        @pl.loop(0, heads)
        def _(head):
            @pl.when(lax.rem(head, sections) == section)
            def _():
                finish(head)

    @pl.when(cross)
    def _():
        for index in range(tokens // ROWS):
            query_place = block * tokens + index * ROWS + lax.broadcasted_iota(
                jnp.int32, (8, ROWS), 1
            )
            start = jnp.zeros((8, ROWS), jnp.int32)
            end = 0
            for document in range(lengths_ref.shape[0]):
                end = end + lengths_ref[document]
                start = jnp.where(query_place >= end, end, start)
            key_place = (
                (block - REACH) * tokens
                + index * ROWS
                + lax.broadcasted_iota(jnp.int32, (span, ROWS), 0)
            )
            allowed = (key_place >= start[:1]) & (key_place <= query_place[:1])
            bias[index] = jnp.where(allowed, 0.0, MASKED_SCORE)

        @pl.when(block < REACH)
        def _():
            for head in range(heads):
                window[head, :, block_rows(0), :] = jnp.zeros((2, tokens, HEAD_SIZE), jnp.bfloat16)

        @pl.when(block == 0)
        def _():
            for head in range(heads):
                window[head, :, block_rows(1), :] = jnp.zeros((2, tokens, HEAD_SIZE), jnp.bfloat16)

        for head in range(heads):
            for kind in range(2):
                load_group(head, kind).wait()

        def pass_on(head):
            first = (2 * place) // (sections + 1)
            for kind in (first, 1 - first):
                ring_copy(head, kind).wait_recv()

                @pl.when(ring_goes_on(kind))
                def _():
                    ring_copy(head, kind).start()

            @pl.when(has_after)
            def _():
                hop_kv(head).start()

            @pl.when(odd == 0)
            def _():
                pair_kv(head, REACH).start()

        def pass_across(head):
            @pl.when(has_before & (odd == 1))
            def _():
                hop_kv(head).wait_recv()
                pair_kv(head, 0).start()

        def compute(head):
            for index in range(tokens // ROWS):
                rows = pl.ds(index * ROWS, ROWS)
                query = jnp.concatenate(
                    [
                        queries[head, rows, member * HEAD_SIZE : (member + 1) * HEAD_SIZE]
                        for member in range(QUERY_PER_KV)
                    ],
                    axis=0,
                )
                cotangent = jnp.concatenate(
                    [
                        cotangents[head, rows, member * HEAD_SIZE : (member + 1) * HEAD_SIZE]
                        for member in range(QUERY_PER_KV)
                    ],
                    axis=0,
                )
                chunks = span // ROWS
                top = jnp.full((8, QUERY_PER_KV * ROWS), -3e38, jnp.float32)
                for chunk in range(chunks):
                    keys = window[head, 0, pl.ds((index + chunk) * ROWS, ROWS), :]
                    mask = bias[index, pl.ds(chunk * ROWS, ROWS), :]
                    score = dot_last(keys, query) + jnp.concatenate([mask] * QUERY_PER_KV, axis=1)
                    score_buf[pl.ds(chunk * ROWS, ROWS), :] = score
                    top = jnp.maximum(top, folded(score, jnp.max))
                top = jnp.max(top, axis=0, keepdims=True)
                total = jnp.zeros((8, QUERY_PER_KV * ROWS), jnp.float32)
                delta = jnp.zeros((8, QUERY_PER_KV * ROWS), jnp.float32)
                for chunk in range(chunks):
                    here = pl.ds(chunk * ROWS, ROWS)
                    values = window[head, 1, pl.ds((index + chunk) * ROWS, ROWS), :]
                    power = jnp.exp2((score_buf[here, :] - top) * exponent_scale)
                    score_buf[here, :] = power
                    prob_grad = dot_last(values, cotangent)
                    prob_grad_buf[here, :] = prob_grad
                    total = total + folded(power, jnp.sum)
                    delta = delta + folded(power * prob_grad, jnp.sum)
                inverse = 1.0 / jnp.sum(total, axis=0, keepdims=True)
                delta = jnp.sum(delta, axis=0, keepdims=True) * inverse
                for chunk in range(chunks):
                    here = pl.ds(chunk * ROWS, ROWS)
                    there = pl.ds((index + chunk) * ROWS, ROWS)
                    prob = score_buf[here, :] * inverse
                    score_grad = prob * (prob_grad_buf[here, :] - delta)
                    key_grad = jnp.dot(
                        score_grad.astype(jnp.bfloat16), query, preferred_element_type=jnp.float32
                    )
                    value_grad = jnp.dot(
                        prob.astype(jnp.bfloat16), cotangent, preferred_element_type=jnp.float32
                    )
                    if index and chunk < chunks - 1:
                        key_grad = key_grad + grads[head, 0, there, :]
                        value_grad = value_grad + grads[head, 1, there, :]
                    grads[head, 0, there, :] = key_grad
                    grads[head, 1, there, :] = value_grad

        def attend(head):
            @pl.when(has_before & (odd == 0))
            def _():
                hop_kv(head).wait_recv()

            @pl.when(has_before | (odd == 1))
            def _():
                pair_kv(head, REACH).wait_recv()

            compute(head)

            @pl.when(has_before | (odd == 1))
            def _():
                pair_grads(head).start()

        def send_back(head):
            @pl.when(has_before)
            def _():
                @pl.when(odd == 0)
                def _():
                    hop_out[head] = grads[head, :, block_rows(0), :].astype(jnp.bfloat16)

                @pl.when(odd == 1)
                def _():
                    pair_grads(head).wait_recv()
                    hop_out[head] = (grads[head, :, block_rows(0), :] + pair_in[head]).astype(
                        jnp.bfloat16
                    )

                hop_grads(head).start()

        def gather(head):
            @pl.when(odd == 0)
            def _():
                pair_grads(head).wait_recv()
                grads[head, :, block_rows(REACH), :] += pair_in[head]

            @pl.when(has_after)
            def _():
                hop_grads(head).wait_recv()
                grads[head, :, block_rows(REACH), :] += hop_in[head].astype(jnp.float32)

            owner = lax.rem(head, sections)

            @pl.when(owner != section)
            def _():
                part_out[head] = grads[head, :, block_rows(REACH), :].astype(jnp.bfloat16)
                part_copy(head, section, owner).start()

        @pl.loop(0, heads + AHEAD + 3)
        def _(step):
            def stage(lag, run):
                head = step - lag

                @pl.when((head >= 0) & (head < heads))
                def _():
                    run(head)

            def finish_own(head):
                @pl.when(lax.rem(head, sections) == section)
                def _():
                    finish(head)

            stage(0, pass_on)
            stage(1, pass_across)
            stage(AHEAD + 1, send_back)
            stage(AHEAD + 2, gather)
            stage(AHEAD + 2, finish_own)
            stage(AHEAD, attend)

    @pl.loop(0, heads)
    def _(head):
        owner = lax.rem(head, sections)
        for kind in range(2):

            @pl.when(owner == section)
            def _():
                store_copy(head, kind).wait()
                for step in range(1, sections):
                    spread_copy(head, kind, lax.rem(section + step, sections)).wait_send()

            @pl.when(owner != section)
            def _():
                spread_copy(head, kind, owner).wait_recv()

            @pl.when(ring_goes_on(kind))
            def _():
                ring_copy(head, kind).wait_send()

        @pl.when(cross)
        def _():
            @pl.when(has_after)
            def _():
                hop_kv(head).wait_send()

            @pl.when(has_before | (odd == 0))
            def _():
                pair_kv(head, REACH).wait_send()

            @pl.when(has_before | (odd == 1))
            def _():
                pair_grads(head).wait_send()

            @pl.when(has_before)
            def _():
                hop_grads(head).wait_send()

            @pl.when(owner != section)
            def _():
                part_copy(head, section, owner).wait_send()


def on_device(projected, grad_out, doc_lengths):
    sections = lax.axis_size("section")
    blocks = lax.axis_size("ctx")
    tokens = projected.shape[1]
    heads = KV_HEAD_COUNT
    slots = -(-heads // sections)
    span = REACH * tokens + ROWS
    window_rows = (REACH + 1) * tokens
    group_width = QUERY_PER_KV * HEAD_SIZE
    bf16, f32 = jnp.bfloat16, jnp.float32
    dma = pltpu.SemaphoreType.DMA
    return pl.pallas_call(
        functools.partial(kernel, sections, blocks),
        out_shape=jax.ShapeDtypeStruct((tokens, 2 * heads * HEAD_SIZE), f32),
        in_specs=[
            pl.BlockSpec(memory_space=pltpu.SMEM),
            pl.BlockSpec(memory_space=pl.ANY),
            pl.BlockSpec(memory_space=pl.ANY),
        ],
        out_specs=pl.BlockSpec(memory_space=pl.ANY),
        scratch_shapes=[
            pltpu.VMEM((heads, tokens, group_width), bf16),
            pltpu.VMEM((heads, tokens, group_width), bf16),
            pltpu.VMEM((heads, 2, window_rows, HEAD_SIZE), bf16),
            pltpu.VMEM((tokens // ROWS, span, ROWS), f32),
            pltpu.VMEM((span, QUERY_PER_KV * ROWS), f32),
            pltpu.VMEM((span, QUERY_PER_KV * ROWS), f32),
            pltpu.VMEM((heads, 2, window_rows, HEAD_SIZE), f32),
            pltpu.VMEM((heads, 2, tokens, HEAD_SIZE), f32),
            pltpu.VMEM((heads, 2, tokens, HEAD_SIZE), bf16),
            pltpu.VMEM((heads, 2, tokens, HEAD_SIZE), bf16),
            pltpu.VMEM((heads, 2, tokens, HEAD_SIZE), bf16),
            pltpu.VMEM((slots, sections, 2, tokens, HEAD_SIZE), bf16),
            pltpu.VMEM((slots, 2, tokens, HEAD_SIZE), f32),
            dma((heads, 2)),
            dma((heads, 2)),
            dma((heads, 2)),
            dma((heads,)),
            dma((heads,)),
            dma((heads,)),
            dma((heads,)),
            dma((heads,)),
            dma((heads,)),
            dma((heads,)),
            dma((heads,)),
            dma((heads,)),
            dma((slots, sections)),
            dma((slots, sections, 2)),
            dma((heads, 2)),
            dma((slots, 2)),
        ],
        compiler_params=pltpu.CompilerParams(
            collective_id=0, has_side_effects=True, vmem_limit_bytes=56 * 1024 * 1024
        ),
        cost_estimate=pl.CostEstimate(
            flops=10 * heads * tokens * group_width * span // 1,
            bytes_accessed=16 * tokens * heads * group_width,
            transcendentals=heads * QUERY_PER_KV * tokens * span,
        ),
    )(doc_lengths, projected[0], grad_out[0])


def solution(mesh):
    return jax.shard_map(
        on_device,
        mesh=mesh,
        in_specs=(P("section", "ctx", None), P("section", "ctx", None), P()),
        out_specs=P("ctx", None),
        check_vma=False,
    )
```

time: 585 us -> 204 us (0.35)
  waiting for transfers between devices: 295 us -> 0 us
  Pallas kernels: 0 us -> 198 us
  matrix products: 140 us -> 0 us
  other arithmetic: 57.2 us -> 0 us
  local copies, waits for them, and re-layouts: 50.4 us -> 3.91 us
  loops' own time: 16.4 us -> 0 us
  between operations: 13.5 us -> 0.01 us
  starting transfers between devices: 9.75 us -> 0 us
    pallas_call x0 -> x1, Pallas kernels: none -> 198 us  [on_device(): pl.pallas_call(functools.partial(kernel, sections, blocks), out_shape=jax...]
    psum x2 -> x0, waiting for transfers between devices: 150 us -> none  [the longest x1 86.4 us: on_device(): return lax.psum(summed, 'section')]
    ppermute x4 -> x0, waiting for transfers between devices: 145 us -> none  [shifted(): lax.ppermute(value, axis, [(source, source + steps) for source in range(l...]
    dot_general x96 -> x0, matrix products: 140 us -> none  [the longest x24 55.7 us: piece_grads(): jnp.einsum('aqk,qah->kh', grad_score, query_group, preferred_element_type...]
    convert_element_type x8 -> x0, other arithmetic: 29.6 us -> none  [group_grads(): attn_half = attn_weight.astype(jnp.bfloat16)]
    another operation x1 -> x0, loops' own time: 16.4 us -> none  [on_device(): lax.map(group_grads, jnp.arange(shared_key_heads, dtype=jnp.int32))]
    dynamic_slice x24 -> x0, local copies, waits for them, and re-layouts: 14.3 us -> none  [the longest x16 9.68 us: group_grads(): lax.dynamic_index_in_dim(grad_heads, kv_index, 1, keepdims=False)]
    slice x10 -> x0, local copies, waits for them, and re-layouts: 12.9 us -> none  [the longest x8 9.65 us: group_grads(): allowed[:, rows]]
  transfers between devices with their start and end apart: 6 -> 0, of which waited for: 5 -> 0; matrix products, arithmetic and copies ran while one was open for 1% -> 0% of each run, Pallas kernels for 0% -> 0%
where the time goes in v1:
time: 204 us; the launch traced here: 202 us
  Pallas kernels  198 us (97%)
  local copies, waits for them, and re-layouts  3.91 us (2%)
    pallas_call x1, Pallas kernels, on_device(): pl.pallas_call(functools.partial(kernel, sections, blocks), out_shape=jax...  198 us

profile of v1, /device:TPU:0, one launch (start us, length us, event | category | flops | bytes accessed | tf_op | source)
XLA Modules:
  0.0 201.9 jit_solution(5538734782074431731)
XLA Ops:
  0.0 198.0 %shard_map.37 = f32[384,2048]{1,0:T(8,128)} custom-call(s32[7]{0:T(128)} %lengths_ref.1, bf16[384,3072]{1,0:T(8,128)(2,1)} %bitcast.2, bf16[384,3072]{1,0:T(8,128)(2,1)} %bitcast.3), custom_call_target="tpu_custom_call" | custom-call | flops 10569646080 | bytes 18874368 | tf_op jit(solution)/shard_map/pallas_call | solution.py:515
  198.0 3.9 %copy.5 = f32[384,2048]{1,0:T(8,128)} copy(f32[384,2048]{1,0:T(8,128)} %shard_map.37) | data formatting | bytes 6291456

commit v2 on v1

--- a/solution.py
+++ b/solution.py
@@ -47,6 +47,7 @@
     bias,
     score_buf,
     prob_grad_buf,
+    halves,
     grads,
     pair_in,
     hop_out,
@@ -334,60 +335,74 @@
                 pair_kv(head, 0).start()
 
         def compute(head):
-            for index in range(tokens // ROWS):
+            chunks = span // ROWS
+
+            def stacked(array, index):
                 rows = pl.ds(index * ROWS, ROWS)
-                query = jnp.concatenate(
+                return jnp.concatenate(
                     [
-                        queries[head, rows, member * HEAD_SIZE : (member + 1) * HEAD_SIZE]
+                        array[head, rows, member * HEAD_SIZE : (member + 1) * HEAD_SIZE]
                         for member in range(QUERY_PER_KV)
                     ],
                     axis=0,
                 )
-                cotangent = jnp.concatenate(
-                    [
-                        cotangents[head, rows, member * HEAD_SIZE : (member + 1) * HEAD_SIZE]
-                        for member in range(QUERY_PER_KV)
-                    ],
-                    axis=0,
+
+            def products(index):
+                band = pl.ds(index * ROWS, span)
+                score_buf[index] = dot_last(window[head, 0, band, :], stacked(queries, index))
+                prob_grad_buf[index] = dot_last(
+                    window[head, 1, band, :], stacked(cotangents, index)
                 )
-                chunks = span // ROWS
+
+            def soften(index):
                 top = jnp.full((8, QUERY_PER_KV * ROWS), -3e38, jnp.float32)
                 for chunk in range(chunks):
-                    keys = window[head, 0, pl.ds((index + chunk) * ROWS, ROWS), :]
-                    mask = bias[index, pl.ds(chunk * ROWS, ROWS), :]
-                    score = dot_last(keys, query) + jnp.concatenate([mask] * QUERY_PER_KV, axis=1)
-                    score_buf[pl.ds(chunk * ROWS, ROWS), :] = score
+                    here = pl.ds(chunk * ROWS, ROWS)
+                    mask = bias[index, here, :]
+                    score = score_buf[index, here, :] + jnp.concatenate(
+                        [mask] * QUERY_PER_KV, axis=1
+                    )
+                    score_buf[index, here, :] = score
                     top = jnp.maximum(top, folded(score, jnp.max))
                 top = jnp.max(top, axis=0, keepdims=True)
                 total = jnp.zeros((8, QUERY_PER_KV * ROWS), jnp.float32)
                 delta = jnp.zeros((8, QUERY_PER_KV * ROWS), jnp.float32)
                 for chunk in range(chunks):
                     here = pl.ds(chunk * ROWS, ROWS)
-                    values = window[head, 1, pl.ds((index + chunk) * ROWS, ROWS), :]
-                    power = jnp.exp2((score_buf[here, :] - top) * exponent_scale)
-                    score_buf[here, :] = power
-                    prob_grad = dot_last(values, cotangent)
-                    prob_grad_buf[here, :] = prob_grad
+                    power = jnp.exp2((score_buf[index, here, :] - top) * exponent_scale)
+                    score_buf[index, here, :] = power
                     total = total + folded(power, jnp.sum)
-                    delta = delta + folded(power * prob_grad, jnp.sum)
+                    delta = delta + folded(power * prob_grad_buf[index, here, :], jnp.sum)
                 inverse = 1.0 / jnp.sum(total, axis=0, keepdims=True)
                 delta = jnp.sum(delta, axis=0, keepdims=True) * inverse
                 for chunk in range(chunks):
                     here = pl.ds(chunk * ROWS, ROWS)
-                    there = pl.ds((index + chunk) * ROWS, ROWS)
-                    prob = score_buf[here, :] * inverse
-                    score_grad = prob * (prob_grad_buf[here, :] - delta)
-                    key_grad = jnp.dot(
-                        score_grad.astype(jnp.bfloat16), query, preferred_element_type=jnp.float32
+                    prob = score_buf[index, here, :] * inverse
+                    score_grad = prob * (prob_grad_buf[index, here, :] - delta)
+                    halves[index, 0, here, :] = score_grad.astype(jnp.bfloat16)
+                    halves[index, 1, here, :] = prob.astype(jnp.bfloat16)
+
+            def accumulate(index):
+                for kind, array in enumerate((queries, cotangents)):
+                    update = jnp.dot(
+                        halves[index, kind],
+                        stacked(array, index),
+                        preferred_element_type=jnp.float32,
                     )
-                    value_grad = jnp.dot(
-                        prob.astype(jnp.bfloat16), cotangent, preferred_element_type=jnp.float32
-                    )
-                    if index and chunk < chunks - 1:
-                        key_grad = key_grad + grads[head, 0, there, :]
-                        value_grad = value_grad + grads[head, 1, there, :]
-                    grads[head, 0, there, :] = key_grad
-                    grads[head, 1, there, :] = value_grad
+                    fresh = span - ROWS if index else 0
+                    if index:
+                        grads[head, kind, pl.ds(index * ROWS, fresh), :] += update[:fresh]
+                    grads[head, kind, pl.ds(index * ROWS + fresh, span - fresh), :] = update[
+                        fresh:
+                    ]
+
+            count = tokens // ROWS
+            products(0)
+            for index in range(count):
+                if index + 1 < count:
+                    products(index + 1)
+                soften(index)
+                accumulate(index)
 
         def attend(head):
             @pl.when(has_before & (odd == 0))
@@ -526,8 +541,9 @@
             pltpu.VMEM((heads, tokens, group_width), bf16),
             pltpu.VMEM((heads, 2, window_rows, HEAD_SIZE), bf16),
             pltpu.VMEM((tokens // ROWS, span, ROWS), f32),
-            pltpu.VMEM((span, QUERY_PER_KV * ROWS), f32),
-            pltpu.VMEM((span, QUERY_PER_KV * ROWS), f32),
+            pltpu.VMEM((tokens // ROWS, span, QUERY_PER_KV * ROWS), f32),
+            pltpu.VMEM((tokens // ROWS, span, QUERY_PER_KV * ROWS), f32),
+            pltpu.VMEM((tokens // ROWS, 2, span, QUERY_PER_KV * ROWS), bf16),
             pltpu.VMEM((heads, 2, window_rows, HEAD_SIZE), f32),
             pltpu.VMEM((heads, 2, tokens, HEAD_SIZE), f32),
             pltpu.VMEM((heads, 2, tokens, HEAD_SIZE), bf16),

time: 204 us -> 202 us (level)
  no operation moved by 1% of the time
where the time goes in v2:
time: 202 us; the launch traced here: 200 us
  Pallas kernels  196 us (97%)
  local copies, waits for them, and re-layouts  3.91 us (2%)
    pallas_call x1, Pallas kernels, on_device(): pl.pallas_call(functools.partial(kernel, sections, blocks), out_shape=jax...  196 us

profile of v2, /device:TPU:0, one launch (start us, length us, event | category | flops | bytes accessed | tf_op | source)
XLA Modules:
  0.0 200.2 jit_solution(9510252150128011522)
XLA Ops:
  0.0 196.3 %shard_map.37 = f32[384,2048]{1,0:T(8,128)} custom-call(s32[7]{0:T(128)} %lengths_ref.1, bf16[384,3072]{1,0:T(8,128)(2,1)} %bitcast.2, bf16[384,3072]{1,0:T(8,128)(2,1)} %bitcast.3), custom_call_target="tpu_custom_call" | custom-call | flops 10569646080 | bytes 18874368 | tf_op jit(solution)/shard_map/pallas_call | solution.py:530
  196.3 3.9 %copy.5 = f32[384,2048]{1,0:T(8,128)} copy(f32[384,2048]{1,0:T(8,128)} %shard_map.37) | data formatting | bytes 6291456

commit v3 on v2

--- a/solution.py
+++ b/solution.py
@@ -55,6 +55,7 @@
     part_out,
     part_in,
     final,
+    final_half,
     load_sem,
     ring_send,
     ring_recv,
@@ -106,20 +107,32 @@
             load_sem.at[head, kind],
         )
 
-    def ring_copy(head, kind):
-        target_place = lax.rem(place + 1 - 2 * kind + sections, sections)
+    def ring_copy(head, kind, way):
+        target_place = lax.rem(place + 1 - 2 * way + sections, sections)
         own = window.at[head, kind, block_rows(REACH), :]
         return pltpu.make_async_remote_copy(
             src_ref=own,
             dst_ref=own,
-            send_sem=ring_send.at[head, kind],
+            send_sem=ring_send.at[head, kind, way],
             recv_sem=ring_recv.at[head, kind],
             device_id={"section": ring_swap(target_place, sections), "ctx": block},
             device_id_type=MESH,
         )
 
-    def ring_goes_on(kind):
-        return lax.rem(place + 1 - 2 * kind + sections, sections) != 0
+    def ring_sends(kind, way):
+        middle = sections // 2
+        if way == 0:
+            return place < middle if kind == 0 else place + 1 < middle
+        above = lax.rem(place - 1 + sections, sections)
+        starts = (place == 0) | (place > middle)
+        return starts & (above > middle if kind == 0 else above >= middle)
+
+    def ring_start(head, kind):
+        for way in range(2):
+
+            @pl.when(ring_sends(kind, way))
+            def _():
+                ring_copy(head, kind, way).start()
 
     def to_block(source, target, send_sem, recv_sem, target_block):
         return pltpu.make_async_remote_copy(
@@ -179,7 +192,7 @@
 
     def spread_copy(head, kind, target):
         return pltpu.make_async_remote_copy(
-            src_ref=final.at[head // sections, kind],
+            src_ref=final_half.at[head // sections, kind],
             dst_ref=out_columns(head, kind),
             send_sem=spread_send.at[head // sections, target, kind],
             recv_sem=spread_recv.at[head, kind],
@@ -189,7 +202,7 @@
 
     def store_copy(head, kind):
         return pltpu.make_async_copy(
-            final.at[head // sections, kind],
+            final_half.at[head // sections, kind],
             out_columns(head, kind),
             store_sem.at[head // sections, kind],
         )
@@ -259,7 +272,8 @@
                 part_copy(head, source, section).wait_recv()
                 final[slot] += part_in[slot, source].astype(jnp.float32)
 
-        final[slot, 0] *= scale
+        final_half[slot, 0] = (final[slot, 0] * scale).astype(jnp.bfloat16)
+        final_half[slot, 1] = final[slot, 1].astype(jnp.bfloat16)
         for kind in range(2):
             store_copy(head, kind).start()
             for step in range(1, sections):
@@ -270,7 +284,7 @@
         for head in range(heads):
             for kind in range(2):
                 load_shared(head, kind).wait()
-                ring_copy(head, kind).start()
+                ring_start(head, kind)
 
         @pl.loop(0, heads)
         def _(head):
@@ -312,13 +326,9 @@
                 load_group(head, kind).wait()
 
         def pass_on(head):
-            first = (2 * place) // (sections + 1)
-            for kind in (first, 1 - first):
-                ring_copy(head, kind).wait_recv()
-
-                @pl.when(ring_goes_on(kind))
-                def _():
-                    ring_copy(head, kind).start()
+            for kind in range(2):
+                ring_copy(head, kind, 0).wait_recv()
+                ring_start(head, kind)
 
             @pl.when(has_after)
             def _():
@@ -453,7 +463,7 @@
                 part_out[head] = grads[head, :, block_rows(REACH), :].astype(jnp.bfloat16)
                 part_copy(head, section, owner).start()
 
-        @pl.loop(0, heads + AHEAD + 3)
+        @pl.loop(0, heads + AHEAD + 4)
         def _(step):
             def stage(lag, run):
                 head = step - lag
@@ -469,10 +479,10 @@
 
             stage(0, pass_on)
             stage(1, pass_across)
+            stage(AHEAD, attend)
             stage(AHEAD + 1, send_back)
             stage(AHEAD + 2, gather)
-            stage(AHEAD + 2, finish_own)
-            stage(AHEAD, attend)
+            stage(AHEAD + 3, finish_own)
 
     @pl.loop(0, heads)
     def _(head):
@@ -489,9 +499,11 @@
             def _():
                 spread_copy(head, kind, owner).wait_recv()
 
-            @pl.when(ring_goes_on(kind))
-            def _():
-                ring_copy(head, kind).wait_send()
+            for way in range(2):
+
+                @pl.when(ring_sends(kind, way))
+                def _():
+                    ring_copy(head, kind, way).wait_send()
 
         @pl.when(cross)
         def _():
@@ -529,7 +541,7 @@
     dma = pltpu.SemaphoreType.DMA
     return pl.pallas_call(
         functools.partial(kernel, sections, blocks),
-        out_shape=jax.ShapeDtypeStruct((tokens, 2 * heads * HEAD_SIZE), f32),
+        out_shape=jax.ShapeDtypeStruct((tokens, 2 * heads * HEAD_SIZE), bf16),
         in_specs=[
             pl.BlockSpec(memory_space=pltpu.SMEM),
             pl.BlockSpec(memory_space=pl.ANY),
@@ -551,8 +563,9 @@
             pltpu.VMEM((heads, 2, tokens, HEAD_SIZE), bf16),
             pltpu.VMEM((slots, sections, 2, tokens, HEAD_SIZE), bf16),
             pltpu.VMEM((slots, 2, tokens, HEAD_SIZE), f32),
+            pltpu.VMEM((slots, 2, tokens, HEAD_SIZE), bf16),
             dma((heads, 2)),
-            dma((heads, 2)),
+            dma((heads, 2, 2)),
             dma((heads, 2)),
             dma((heads,)),
             dma((heads,)),
@@ -576,7 +589,7 @@
             bytes_accessed=16 * tokens * heads * group_width,
             transcendentals=heads * QUERY_PER_KV * tokens * span,
         ),
-    )(doc_lengths, projected[0], grad_out[0])
+    )(doc_lengths, projected[0], grad_out[0]).astype(f32)
 
 
 def solution(mesh):

time: 202 us -> 103 us (0.51)
  Pallas kernels: 196 us -> 99.5 us
  local copies, waits for them, and re-layouts: 3.91 us -> 0 us
  other arithmetic: 0 us -> 3.45 us
    pallas_call x1, Pallas kernels: 196 us -> 99.5 us  [on_device(): pl.pallas_call(functools.partial(kernel, sections, blocks), out_shape=jax...]
    unnamed x1 -> x0, local copies, waits for them, and re-layouts: 3.91 us -> none
    convert_element_type x0 -> x1, other arithmetic: none -> 3.45 us  [on_device(): return pl.pallas_call(functools.partial(kernel, sections, blocks), out_sh...]
where the time goes in v3:
time: 103 us
  Pallas kernels  99.5 us (97%)
  other arithmetic  3.45 us (3%)
    pallas_call x1, Pallas kernels, on_device(): pl.pallas_call(functools.partial(kernel, sections, blocks), out_shape=jax...  99.5 us
    convert_element_type x1, other arithmetic, on_device(): return pl.pallas_call(functools.partial(kernel, sections, blocks), out_sh...  3.45 us

profile of v3, /device:TPU:0, one launch (start us, length us, event | category | flops | bytes accessed | tf_op | source)
XLA Modules:
  0.0 103.0 jit_solution(16234521586118484532)
XLA Ops:
  0.0 99.5 %shard_map.37 = bf16[384,2048]{1,0:T(8,128)(2,1)} custom-call(s32[7]{0:T(128)} %lengths_ref.1, bf16[384,3072]{1,0:T(8,128)(2,1)} %bitcast.2, bf16[384,3072]{1,0:T(8,128)(2,1)} %bitcast.3), custom_call_target="tpu_custom_call" | custom-call | flops 10569646080 | bytes 18874368 | tf_op jit(solution)/shard_map/pallas_call | solution.py:542
  99.5 3.4 %convert_element_type.3 = f32[384,2048]{1,0:T(8,128)} convert(bf16[384,2048]{1,0:T(8,128)(2,1)} %shard_map.37) | non-fusion elementwise | flops 786432 | bytes 4718592 | tf_op jit(solution)/shard_map/convert_element_type | solution.py:592
